TPU v7x, 512 devices: a whole 4x8x8 slice. The times are simulated.
512 devices in a mesh: smp: 8 (over x, y_hi), proto: 64 (over y_lo, z, core).
Axes of the slice: x: 4, y: 8 (y_hi: 2, y_lo: 4; y = y_hi * 4 + y_lo), z: 8, core: 2. Of those that a mesh axis runs over, the one named last changes fastest.
Arguments:
- teacher_features: bfloat16 [1024, 512], P('smp', 'proto'), may hold values from -6 to 6
- student_features: bfloat16 [1024, 512], P('smp', 'proto'), may hold values from -6 to 6
- teacher_weight: bfloat16 [131072, 512], P('proto'), may hold values from -0.45 to 0.45
- student_weight: bfloat16 [131072, 512], P('proto'), may hold values from -0.19921875 to 0.19921875
Outputs:
- sample_loss: float32 [1024], P('smp')
- grad_features: float32 [1024, 512], P('smp', 'proto')
- grad_weight: float32 [131072, 512], P('proto', 'smp')
All inputs are finite; a program needn't handle non-finite values.
Results may differ from a plain program's by a relative error of at most 0.0085.
Values may be sent and summed in bfloat16 or wider, within the bound.
No kernel may reach another device: no remote copies, remote signals or barrier semaphores. Data moves between devices by JAX's collectives and lax.ppermute only.
A program may use at most 64 MiB of HBM per device.

v0:
```python
import jax
import jax.numpy as jnp
from jax import lax
from jax.sharding import PartitionSpec as P

ITERS = 3
TEACHER_TEMP = 0.07
STUDENT_TEMP = 0.1


def sent_to_all(x, axis):
    count = lax.axis_size(axis)
    return lax.all_to_all(jnp.broadcast_to(x[None], (count, *x.shape)), axis, 0, 0, tiled=True)


def taken_together(x, axis):
    return sent_to_all(x, axis).sum(axis=0)


def packed_total(arrays, axis):
    flat, at, done = (jnp.concatenate([a.reshape(-1) for a in arrays]), 0, [])
    total = taken_together(flat, axis)
    for a in arrays:
        done.append(total[at : at + a.size].reshape(a.shape))
        at += a.size
    return tuple(done)


def turned_gather(arrays, axis, dims):
    turned = [jnp.moveaxis(a, dim, 0) for a, dim in zip(arrays, dims)]
    widths = [t[0].size for t in turned]
    both = jnp.concatenate([t.reshape(-1, w) for t, w in zip(turned, widths)], axis=1)
    whole = lax.all_gather(both, axis, axis=0, tiled=True)
    pieces = jnp.split(whole, [sum(widths[:k]) for k in range(1, len(widths))], axis=1)
    return tuple(
        (
            jnp.moveaxis(b.reshape(-1, *t.shape[1:]), 0, dim)
            for b, t, dim in zip(pieces, turned, dims)
        )
    )


def cut_along(x, dim, count):
    before, after = (x.shape[:dim], x.shape[dim + 1 :])
    return jnp.moveaxis(x.reshape(*before, count, -1, *after), dim, 0)


def sent_and_summed(x, axis, dim):
    count = lax.axis_size(axis)
    pieces = lax.all_to_all(cut_along(x, dim, count), axis, 0, 0, tiled=True)
    return jnp.sum(pieces.astype(jnp.float32), axis=0)


def sum_at_owner(x, axis, dim):
    pieces = cut_along(x, dim, lax.axis_size(axis))
    arrived = lax.all_to_all(pieces, axis, split_axis=0, concat_axis=0, tiled=True)
    return arrived.sum(axis=0)


def unit_rows(features):
    values = features.astype(jnp.float32)
    scale = lax.rsqrt(jnp.sum(values * values, axis=1) + 1e-06)
    return ((values * scale[:, None]).astype(jnp.bfloat16), scale)


def project(rows, weight):
    return lax.dot_general(
        rows, weight, (((1,), (1,)), ((), ())), preferred_element_type=jnp.float32
    )


def sample_totals(values):
    return (taken_together(values[0], "proto"),)


def student_totals(values):
    return packed_total((values[0], values[1]), "proto")


def on_device(teacher_features, student_features, teacher_weight, student_weight):
    teacher_all, student_all = turned_gather((teacher_features, student_features), "proto", (1, 1))
    sample_rows = teacher_features.shape[0]
    proto_rows = teacher_weight.shape[0]
    samples = sample_rows * lax.axis_size("smp")
    protos = proto_rows * lax.axis_size("proto")
    teacher_unit, unused = unit_rows(teacher_all)
    student_unit, student_scale = unit_rows(student_all)
    kernel = jnp.exp(project(teacher_unit, teacher_weight) / TEACHER_TEMP)
    col_scale = jnp.ones((sample_rows,), jnp.float32)
    row_scale = jnp.ones((proto_rows,), jnp.float32)
    exp_total = None
    for step in range(ITERS):
        proto_mass = jnp.dot(col_scale, kernel, precision=lax.Precision.HIGHEST)
        row_scale = 1.0 / (protos * taken_together(proto_mass, "smp"))
        sample_part = jnp.dot(kernel, row_scale, precision=lax.Precision.HIGHEST)
        sample_mass = sample_totals((sample_part,))[0]
        col_scale = 1.0 / (samples * sample_mass)
    targets = samples * kernel * row_scale[None, :] * col_scale[:, None]
    logits = project(student_unit, student_weight) / STUDENT_TEMP
    expo = jnp.exp(logits)
    logits, expo, local_total = (logits, expo, jnp.sum(expo, axis=1))
    weighted = jnp.sum(targets * logits, axis=1)
    exp_total, weighted_total = student_totals((local_total, weighted))
    probs = expo / exp_total[:, None]
    sample_loss = jnp.log(exp_total) - weighted_total
    logit_grad = ((probs - targets) / (samples * STUDENT_TEMP)).astype(jnp.bfloat16)
    weight_part = lax.dot_general(
        logit_grad, student_unit, (((0,), (0,)), ((), ())), preferred_element_type=jnp.float32
    )
    grad_weight = sent_and_summed(weight_part.astype(jnp.bfloat16), "smp", 1)
    unit_part = jnp.dot(logit_grad, student_weight, preferred_element_type=jnp.float32)
    unit_grad = sum_at_owner(unit_part, "proto", 1)
    feats = student_features.astype(jnp.float32)
    inner_prod = taken_together(jnp.sum(feats * unit_grad, axis=1), "proto")
    grad_features = (
        student_scale[:, None] * unit_grad - (student_scale**3 * inner_prod)[:, None] * feats
    )
    return (sample_loss, grad_features, grad_weight)


def solution(mesh):
    placed = (P("smp", "proto"), P("smp", "proto"), P("proto", None), P("proto", None))
    return jax.shard_map(
        on_device,
        mesh=mesh,
        in_specs=placed,
        out_specs=(P("smp"), P("smp", "proto"), P("proto", "smp")),
        check_vma=False,
    )
```

profile of v0, /device:TPU:8, one launch (start us, length us, event | category | flops | bytes accessed | tf_op | source)
XLA Modules:
  0.0 290.4 jit_solution(18363776780646376817)
XLA Ops:
  0.6 0.9 pad_maximum_fusion
  1.5 71.8 %all_gather.3 = bf16[512,256]{1,0:T(8,128)(2,1)S(1)} all-gather(bf16[8,256]{1,0:T(8,128)(2,1)S(1)} %pad_maximum_fusion), channel_id=1, replica_groups=mesh['smp'=8,'proto'=64] {'proto'}, dimensions={0}, use_global_device_ids=true | all-gather | bytes 266240 | tf_op jit(solution)/shard_map/all_gather | solution.py:33
  73.4 2.4 fusion
  75.8 0.6 fusion.21
  76.5 17.3 %all_to_all.58 = f32[8,1,2048]{2,1,0:T(1,128)S(1)} all-to-all(f32[8,1,2048]{2,1,0:T(1,128)S(1)} %broadcast_in_dim.16), channel_id=1, replica_groups=mesh['smp'=8,'proto'=64] {'smp'}, dimensions={0} | all-to-all | bytes 131072 | tf_op jit(solution)/shard_map/all_to_all | solution.py:13
  93.8 0.9 convolution_bitcast_fusion.3
  94.8 27.2 %all_to_all.59 = f32[64,1,128]{2,1,0:T(1,128)S(1)} all-to-all(f32[64,1,128]{2,1,0:T(1,128)S(1)} %broadcast_in_dim.17), channel_id=1, replica_groups=mesh['smp'=8,'proto'=64] {'proto'}, dimensions={0} | all-to-all | bytes 65536 | tf_op jit(solution)/shard_map/all_to_all | solution.py:13
  122.0 0.6 fusion.15
  122.6 12.9 %all_to_all.60 = f32[8,1,2048]{2,1,0:T(1,128)S(1)} all-to-all(f32[8,1,2048]{2,1,0:T(1,128)S(1)} %broadcast_in_dim.18), channel_id=1, replica_groups=mesh['smp'=8,'proto'=64] {'smp'}, dimensions={0} | all-to-all | bytes 131072 | tf_op jit(solution)/shard_map/all_to_all | solution.py:13
  135.6 0.9 convolution_bitcast_fusion.2
  136.6 13.4 %all_to_all.61 = f32[64,1,128]{2,1,0:T(1,128)S(1)} all-to-all(f32[64,1,128]{2,1,0:T(1,128)S(1)} %broadcast_in_dim.19), channel_id=1, replica_groups=mesh['smp'=8,'proto'=64] {'proto'}, dimensions={0} | all-to-all | bytes 65536 | tf_op jit(solution)/shard_map/all_to_all | solution.py:13
  150.0 0.6 fusion.13
  150.6 12.9 %all_to_all.62 = f32[8,1,2048]{2,1,0:T(1,128)S(1)} all-to-all(f32[8,1,2048]{2,1,0:T(1,128)S(1)} %broadcast_in_dim.20), channel_id=1, replica_groups=mesh['smp'=8,'proto'=64] {'smp'}, dimensions={0} | all-to-all | bytes 131072 | tf_op jit(solution)/shard_map/all_to_all | solution.py:13
  163.6 0.9 convolution_bitcast_fusion.1
  164.6 13.4 %all_to_all.63 = f32[64,1,128]{2,1,0:T(1,128)S(1)} all-to-all(f32[64,1,128]{2,1,0:T(1,128)S(1)} %broadcast_in_dim.21), channel_id=1, replica_groups=mesh['smp'=8,'proto'=64] {'proto'}, dimensions={0} | all-to-all | bytes 65536 | tf_op jit(solution)/shard_map/all_to_all | solution.py:13
  178.0 1.8 exponential_reduce_fusion
  179.9 13.7 %all_to_all.64 = f32[64,1,256]{2,1,0:T(1,128)S(1)} all-to-all(f32[64,1,256]{2,1,0:T(1,128)S(1)} %broadcast_in_dim.22), channel_id=1, replica_groups=mesh['smp'=8,'proto'=64] {'proto'}, dimensions={0} | all-to-all | bytes 131072 | tf_op jit(solution)/shard_map/all_to_all | solution.py:13
  193.6 0.1 reduce_sum.145
  193.7 0.5 fusion.32
  194.2 1.5 multiply_convert_fusion
  195.8 0.8 copy-done.1
  196.6 0.9 convolution_bitcast_fusion
  197.5 16.8 %all_to_all.65 = f32[64,128,8]{1,2,0:T(8,128)S(1)} all-to-all(f32[64,128,8]{1,2,0:T(8,128)S(1)} %convolution_bitcast_fusion), channel_id=1, replica_groups=mesh['smp'=8,'proto'=64] {'proto'}, dimensions={0} | all-to-all | bytes 524288 | tf_op jit(solution)/shard_map/all_to_all | solution.py:56
  214.3 0.1 reduce_sum.146
  214.4 0.6 broadcast_in_dim.23
  215.0 5.7 %all-to-all-start.8 = ((f32[64,1,128]{2,1,0:T(1,128)}), f32[64,1,128]{2,1,0:T(1,128)S(1)}, u32[]{:S(2)}, u32[]{:S(2)}) async-start(f32[64,1,128]{2,1,0:T(1,128)} %broadcast_in_dim.23), calls=%async_computation.8 | async-start | bytes 65536 | tf_op jit(solution)/shard_map/all_to_all | solution.py:13
  220.7 3.1 %convolution_convert_fusion = bf16[2048,512]{0,1:T(8,128)(2,1)} fusion(bf16[128,2048]{1,0:T(8,128)(2,1)} %copy-done.1, f32[128]{0:T(128)S(1)} %get-tuple-element.13, bf16[512,256]{1,0:T(8,128)(2,1)S(1)} %all_gather.3), kind=kOutput, calls=%fused_computation.1 | convolution fusion | flops 269680640 | bytes 2753024 | tf_op jit(solution)/shard_map/dot_general | solution.py:107
  223.8 5.8 %all-to-all-done.8 = f32[64,1,128]{2,1,0:T(1,128)S(1)} async-done(((f32[64,1,128]{2,1,0:T(1,128)}), f32[64,1,128]{2,1,0:T(1,128)S(1)}, u32[]{:S(2)}, u32[]{:S(2)}) %all-to-all-start.8) | async-done | bytes 32800 | tf_op jit(solution)/shard_map/all_to_all | solution.py:13
  229.6 4.4 %all-to-all-start.9 = ((bf16[8,2048,64]{1,2,0:T(8,128)(2,1)}), bf16[8,2048,64]{1,2,0:T(8,128)(2,1)}, u32[]{:S(2)}, u32[]{:S(2)}) async-start(bf16[8,2048,64]{1,2,0:T(8,128)(2,1)} %bitcast.45), calls=%async_computation.9 | async-start | bytes 4194304 | tf_op jit(solution)/shard_map/all_to_all | solution.py:50
  234.0 0.6 fusion.11
  234.6 53.0 %all-to-all-done.9 = bf16[8,2048,64]{1,2,0:T(8,128)(2,1)} async-done(((bf16[8,2048,64]{1,2,0:T(8,128)(2,1)}), bf16[8,2048,64]{1,2,0:T(8,128)(2,1)}, u32[]{:S(2)}, u32[]{:S(2)}) %all-to-all-start.9) | async-done | bytes 2097184 | tf_op jit(solution)/shard_map/all_to_all | solution.py:50
  287.6 2.8 convert_reduce_fusion
  (28 shorter events, 0.7 us)
Async XLA Ops:
  0.6 177.3 %copy-start = (bf16[2048,512]{1,0:T(8,128)(2,1)S(1)}, bf16[2048,512]{1,0:T(8,128)(2,1)}, u32[]{:S(2)}) copy-start(bf16[2048,512]{1,0:T(8,128)(2,1)} %param.7) | copy-start | bytes 6291460
  195.8 0.8 copy-start.1
  196.6 17.8 %copy-start.2 = (bf16[128,8]{0,1:T(8,128)(2,1)S(1)}, bf16[128,8]{0,1:T(8,128)(2,1)}, u32[]{:S(2)}) copy-start(bf16[128,8]{0,1:T(8,128)(2,1)} %param.5) | copy-start | bytes 6148
  215.0 14.5 %all-to-all-start.8 = ((f32[64,1,128]{2,1,0:T(1,128)}), f32[64,1,128]{2,1,0:T(1,128)S(1)}, u32[]{:S(2)}, u32[]{:S(2)}) async-start(f32[64,1,128]{2,1,0:T(1,128)} %broadcast_in_dim.23), calls=%async_computation.8 | async-start | bytes 65536 | tf_op jit(solution)/shard_map/all_to_all | solution.py:13
  229.6 58.0 %all-to-all-start.9 = ((bf16[8,2048,64]{1,2,0:T(8,128)(2,1)}), bf16[8,2048,64]{1,2,0:T(8,128)(2,1)}, u32[]{:S(2)}, u32[]{:S(2)}) async-start(bf16[8,2048,64]{1,2,0:T(8,128)(2,1)} %bitcast.45), calls=%async_computation.9 | async-start | bytes 4194304 | tf_op jit(solution)/shard_map/all_to_all | solution.py:50
where the time goes:
time: 291 us; the launch traced here: 290 us
  blocking collectives  199 us (68%)
  waiting for transfers between devices  58.8 us (20%)
  matrix products  12.9 us (4%)
  starting transfers between devices  10 us (3%)
  other arithmetic  6.86 us (2%)
    all_to_all x7, blocking collectives, sent_to_all(): lax.all_to_all(jnp.broadcast_to(x[None], (count, *x.shape)), axis, 0, 0,...  111 us
    all_gather x1, blocking collectives, turned_gather(): whole = lax.all_gather(both, axis, axis=0, tiled=True)  71.8 us
    all_to_all x1, waiting for transfers between devices, sent_and_summed(): pieces = lax.all_to_all(cut_along(x, dim, count), axis, 0, 0, tiled=True)  53 us
    all_to_all x1, blocking collectives, sum_at_owner(): lax.all_to_all(pieces, axis, split_axis=0, concat_axis=0, tiled=True)  16.8 us
  transfers between devices with their start and end apart: 2, of which 2 were waited for; matrix products, arithmetic and copies ran while one was open for 1% of the time, Pallas kernels for 0%

commit v1 on v0

--- a/solution.py
+++ b/solution.py
@@ -30,7 +30,9 @@
     turned = [jnp.moveaxis(a, dim, 0) for a, dim in zip(arrays, dims)]
     widths = [t[0].size for t in turned]
     both = jnp.concatenate([t.reshape(-1, w) for t, w in zip(turned, widths)], axis=1)
-    whole = lax.all_gather(both, axis, axis=0, tiled=True)
+    whole = jnp.concatenate(
+        lax.all_to_all(jnp.stack([both] * lax.axis_size(axis)), axis, 0, 0), axis=0
+    )
     pieces = jnp.split(whole, [sum(widths[:k]) for k in range(1, len(widths))], axis=1)
     return tuple(
         (

time: 291 us -> 232 us (0.80)
  blocking collectives: 199 us -> 140 us
    all_gather x1 -> x0, blocking collectives: 71.8 us -> none  [turned_gather(): whole = lax.all_gather(both, axis, axis=0, tiled=True)]
    all_to_all x0 -> x1, blocking collectives: none -> 26.1 us  [turned_gather(): lax.all_to_all(jnp.stack([both] * lax.axis_size(axis)), axis, 0, 0)]
    all_to_all x7, blocking collectives: 111 us -> 97.6 us  [sent_to_all(): lax.all_to_all(jnp.broadcast_to(x[None], (count, *x.shape)), axis, 0, 0,...]
  transfers between devices with their start and end apart: 2 -> 2, of which waited for: 2 -> 2; matrix products, arithmetic and copies ran while one was open for 1% -> 2% of each run, Pallas kernels for 0% -> 0%
where the time goes in v1:
time: 232 us; the launch traced here: 231 us
  blocking collectives  140 us (60%)
  waiting for transfers between devices  58.8 us (25%)
  matrix products  12.9 us (6%)
  starting transfers between devices  10 us (4%)
  other arithmetic  6.86 us (3%)
    all_to_all x7, blocking collectives, sent_to_all(): lax.all_to_all(jnp.broadcast_to(x[None], (count, *x.shape)), axis, 0, 0,...  97.6 us
    all_to_all x1, waiting for transfers between devices, sent_and_summed(): pieces = lax.all_to_all(cut_along(x, dim, count), axis, 0, 0, tiled=True)  53 us
    all_to_all x1, blocking collectives, turned_gather(): lax.all_to_all(jnp.stack([both] * lax.axis_size(axis)), axis, 0, 0)  26.1 us
    all_to_all x1, blocking collectives, sum_at_owner(): lax.all_to_all(pieces, axis, split_axis=0, concat_axis=0, tiled=True)  16.6 us
    all_to_all x1, waiting for transfers between devices, sent_to_all(): lax.all_to_all(jnp.broadcast_to(x[None], (count, *x.shape)), axis, 0, 0,...  5.78 us
    all_to_all x1, starting transfers between devices, sent_to_all(): lax.all_to_all(jnp.broadcast_to(x[None], (count, *x.shape)), axis, 0, 0,...  5.66 us
  transfers between devices with their start and end apart: 2, of which 2 were waited for; matrix products, arithmetic and copies ran while one was open for 2% of the time, Pallas kernels for 0%

profile of v1, /device:TPU:8, one launch (start us, length us, event | category | flops | bytes accessed | tf_op | source)
XLA Modules:
  0.0 231.3 jit_solution(14418264967514713911)
XLA Ops:
  0.6 0.9 pad_maximum_fusion
  1.5 26.1 %all_to_all.63 = bf16[64,8,256]{2,1,0:T(8,128)(2,1)S(1)} all-to-all(bf16[64,8,256]{2,1,0:T(8,128)(2,1)S(1)} %stack.2), channel_id=1, replica_groups=mesh['smp'=8,'proto'=64] {'proto'}, dimensions={0} | all-to-all | bytes 524288 | tf_op jit(solution)/shard_map/all_to_all | solution.py:34
  27.7 2.4 %fusion = f32[128,2048]{1,0:T(8,128)S(1)} fusion(bf16[2048,512]{1,0:T(8,128)(2,1)} %param.6, f32[128]{0:T(128)S(1)} %get-tuple-element.12, bf16[512,256]{1,0:T(8,128)(2,1)S(1)} %bitcast.48), kind=kOutput, calls=%fused_computation.3 | convolution fusion | flops 268894208 | bytes 3277312 | tf_op jit(solution)/shard_map/dot_general | solution.py:69
  30.2 0.6 fusion.21
  30.8 16.9 %all_to_all.64 = f32[8,1,2048]{2,1,0:T(1,128)S(1)} all-to-all(f32[8,1,2048]{2,1,0:T(1,128)S(1)} %broadcast_in_dim.16), channel_id=1, replica_groups=mesh['smp'=8,'proto'=64] {'smp'}, dimensions={0} | all-to-all | bytes 131072 | tf_op jit(solution)/shard_map/all_to_all | solution.py:13
  47.8 0.9 convolution_bitcast_fusion.3
  48.7 14.3 %all_to_all.65 = f32[64,1,128]{2,1,0:T(1,128)S(1)} all-to-all(f32[64,1,128]{2,1,0:T(1,128)S(1)} %broadcast_in_dim.17), channel_id=1, replica_groups=mesh['smp'=8,'proto'=64] {'proto'}, dimensions={0} | all-to-all | bytes 65536 | tf_op jit(solution)/shard_map/all_to_all | solution.py:13
  63.1 0.6 fusion.15
  63.8 12.9 %all_to_all.66 = f32[8,1,2048]{2,1,0:T(1,128)S(1)} all-to-all(f32[8,1,2048]{2,1,0:T(1,128)S(1)} %broadcast_in_dim.18), channel_id=1, replica_groups=mesh['smp'=8,'proto'=64] {'smp'}, dimensions={0} | all-to-all | bytes 131072 | tf_op jit(solution)/shard_map/all_to_all | solution.py:13
  76.7 0.9 convolution_bitcast_fusion.2
  77.7 13.4 %all_to_all.67 = f32[64,1,128]{2,1,0:T(1,128)S(1)} all-to-all(f32[64,1,128]{2,1,0:T(1,128)S(1)} %broadcast_in_dim.19), channel_id=1, replica_groups=mesh['smp'=8,'proto'=64] {'proto'}, dimensions={0} | all-to-all | bytes 65536 | tf_op jit(solution)/shard_map/all_to_all | solution.py:13
  91.1 0.6 fusion.13
  91.7 12.9 %all_to_all.68 = f32[8,1,2048]{2,1,0:T(1,128)S(1)} all-to-all(f32[8,1,2048]{2,1,0:T(1,128)S(1)} %broadcast_in_dim.20), channel_id=1, replica_groups=mesh['smp'=8,'proto'=64] {'smp'}, dimensions={0} | all-to-all | bytes 131072 | tf_op jit(solution)/shard_map/all_to_all | solution.py:13
  104.7 0.9 convolution_bitcast_fusion.1
  105.7 13.4 %all_to_all.69 = f32[64,1,128]{2,1,0:T(1,128)S(1)} all-to-all(f32[64,1,128]{2,1,0:T(1,128)S(1)} %broadcast_in_dim.21), channel_id=1, replica_groups=mesh['smp'=8,'proto'=64] {'proto'}, dimensions={0} | all-to-all | bytes 65536 | tf_op jit(solution)/shard_map/all_to_all | solution.py:13
  119.1 1.8 exponential_reduce_fusion
  121.0 13.7 %all_to_all.70 = f32[64,1,256]{2,1,0:T(1,128)S(1)} all-to-all(f32[64,1,256]{2,1,0:T(1,128)S(1)} %broadcast_in_dim.22), channel_id=1, replica_groups=mesh['smp'=8,'proto'=64] {'proto'}, dimensions={0} | all-to-all | bytes 131072 | tf_op jit(solution)/shard_map/all_to_all | solution.py:13
  134.7 0.1 reduce_sum.145
  134.8 0.5 fusion.32
  135.3 1.5 multiply_convert_fusion
  136.9 0.8 copy-done.1
  137.7 0.9 convolution_bitcast_fusion
  138.6 16.6 %all_to_all.71 = f32[64,128,8]{1,2,0:T(8,128)S(1)} all-to-all(f32[64,128,8]{1,2,0:T(8,128)S(1)} %convolution_bitcast_fusion), channel_id=1, replica_groups=mesh['smp'=8,'proto'=64] {'proto'}, dimensions={0} | all-to-all | bytes 524288 | tf_op jit(solution)/shard_map/all_to_all | solution.py:58
  155.3 0.1 reduce_sum.146
  155.4 0.6 broadcast_in_dim.23
  156.0 5.7 %all-to-all-start.9 = ((f32[64,1,128]{2,1,0:T(1,128)}), f32[64,1,128]{2,1,0:T(1,128)S(1)}, u32[]{:S(2)}, u32[]{:S(2)}) async-start(f32[64,1,128]{2,1,0:T(1,128)} %broadcast_in_dim.23), calls=%async_computation.9 | async-start | bytes 65536 | tf_op jit(solution)/shard_map/all_to_all | solution.py:13
  161.6 3.1 %convolution_convert_fusion = bf16[2048,512]{0,1:T(8,128)(2,1)} fusion(bf16[128,2048]{1,0:T(8,128)(2,1)} %copy-done.1, f32[128]{0:T(128)S(1)} %get-tuple-element.13, bf16[512,256]{1,0:T(8,128)(2,1)S(1)} %bitcast.50), kind=kOutput, calls=%fused_computation.1 | convolution fusion | flops 269680640 | bytes 2753024 | tf_op jit(solution)/shard_map/dot_general | solution.py:109
  164.7 5.8 %all-to-all-done.9 = f32[64,1,128]{2,1,0:T(1,128)S(1)} async-done(((f32[64,1,128]{2,1,0:T(1,128)}), f32[64,1,128]{2,1,0:T(1,128)S(1)}, u32[]{:S(2)}, u32[]{:S(2)}) %all-to-all-start.9) | async-done | bytes 32800 | tf_op jit(solution)/shard_map/all_to_all | solution.py:13
  170.5 4.4 %all-to-all-start.10 = ((bf16[8,2048,64]{1,2,0:T(8,128)(2,1)}), bf16[8,2048,64]{1,2,0:T(8,128)(2,1)}, u32[]{:S(2)}, u32[]{:S(2)}) async-start(bf16[8,2048,64]{1,2,0:T(8,128)(2,1)} %bitcast.46), calls=%async_computation.10 | async-start | bytes 4194304 | tf_op jit(solution)/shard_map/all_to_all | solution.py:52
  174.9 0.6 fusion.11
  175.5 53.0 %all-to-all-done.10 = bf16[8,2048,64]{1,2,0:T(8,128)(2,1)} async-done(((bf16[8,2048,64]{1,2,0:T(8,128)(2,1)}), bf16[8,2048,64]{1,2,0:T(8,128)(2,1)}, u32[]{:S(2)}, u32[]{:S(2)}) %all-to-all-start.10) | async-done | bytes 2097184 | tf_op jit(solution)/shard_map/all_to_all | solution.py:52
  228.6 2.8 %convert_reduce_fusion = f32[2048,64]{0,1:T(8,128)} fusion(bf16[8,2048,64]{1,2,0:T(8,128)(2,1)} %all-to-all-done.10), kind=kLoop, calls=%fused_computation | loop fusion | flops 1966080 | bytes 2621440 | tf_op jit(solution)/shard_map/reduce_sum | solution.py:53
  (29 shorter events, 0.7 us)
Async XLA Ops:
  0.6 118.5 %copy-start = (bf16[2048,512]{1,0:T(8,128)(2,1)S(1)}, bf16[2048,512]{1,0:T(8,128)(2,1)}, u32[]{:S(2)}) copy-start(bf16[2048,512]{1,0:T(8,128)(2,1)} %param.7) | copy-start | bytes 6291460
  136.9 0.8 copy-start.1
  137.7 17.7 %copy-start.2 = (bf16[128,8]{0,1:T(8,128)(2,1)S(1)}, bf16[128,8]{0,1:T(8,128)(2,1)}, u32[]{:S(2)}) copy-start(bf16[128,8]{0,1:T(8,128)(2,1)} %param.5) | copy-start | bytes 6148
  156.0 14.5 %all-to-all-start.9 = ((f32[64,1,128]{2,1,0:T(1,128)}), f32[64,1,128]{2,1,0:T(1,128)S(1)}, u32[]{:S(2)}, u32[]{:S(2)}) async-start(f32[64,1,128]{2,1,0:T(1,128)} %broadcast_in_dim.23), calls=%async_computation.9 | async-start | bytes 65536 | tf_op jit(solution)/shard_map/all_to_all | solution.py:13
  170.5 58.0 %all-to-all-start.10 = ((bf16[8,2048,64]{1,2,0:T(8,128)(2,1)}), bf16[8,2048,64]{1,2,0:T(8,128)(2,1)}, u32[]{:S(2)}, u32[]{:S(2)}) async-start(bf16[8,2048,64]{1,2,0:T(8,128)(2,1)} %bitcast.46), calls=%async_computation.10 | async-start | bytes 4194304 | tf_op jit(solution)/shard_map/all_to_all | solution.py:52
